TPU v7x, 256 devices: a whole 4x4x8 slice. The times are simulated.
256 devices in a mesh: dp: 64 (over z, y, x_hi), seq: 4 (over x_lo, core).
Axes of the slice: x: 4 (x_hi: 2, x_lo: 2; x = x_hi * 2 + x_lo), y: 4, z: 8, core: 2. Of those that a mesh axis runs over, the one named last changes fastest.
Arguments:
- queries: bfloat16 [64, 1024, 1024], P('dp', 'seq'), may hold values from -5 to 5
- keys: bfloat16 [64, 1024, 1024], P('dp', 'seq'), may hold values from -5 to 5
- values: bfloat16 [64, 1024, 1024], P('dp', 'seq'), may hold values from -16 to 16
- segment_ids: int32 [64, 1024], P('dp', 'seq'), may hold values from 0 to 7, never falling along the last dimension, each value on 1 to 512 neighbouring positions
- out_weight: bfloat16 [1024, 2048], replicated, may hold values from -0.1875 to 0.1875
- out_grad: bfloat16 [64, 1024, 2048], P('dp', 'seq'), may hold values from -6 to 6
Outputs:
- projected: bfloat16 [64, 1024, 2048], P('dp', 'seq')
- query_grad: bfloat16 [64, 1024, 1024], P('dp', 'seq')
- key_grad: bfloat16 [64, 1024, 1024], P('dp', 'seq')
- value_grad: bfloat16 [64, 1024, 1024], P('dp', 'seq')
- weight_grad: bfloat16 [1024, 2048], P('dp')
Inputs may be any that keep to these rules, and one draw needn't show every extreme that they name: `segment_ids`: each row holds 8 documents in order, the longest exactly 512 positions.
All inputs are finite; a program needn't handle non-finite values.
Results may differ from a plain program's by a relative error of at most 0.029.
Values may be sent and summed in bfloat16 or wider, within the bound.
A program may use at most 128 MiB of HBM per device.

v0:
```python
import jax
import jax.numpy as jnp
from jax import lax
from jax.sharding import PartitionSpec as P

HEAD = 128


def attention_weights(query_heads, key_heads, query_places, key_places, query_docs, key_docs):
    scores = jnp.einsum(
        "qhe,khe->hqk", query_heads, key_heads, preferred_element_type=jnp.float32
    ) * HEAD ** (-0.5)
    visible = (key_places[None, :] <= query_places[:, None]) & (
        query_docs[:, None] == key_docs[None, :]
    )
    scores = jnp.where(visible[None], scores, -1e30)
    row_top = jnp.max(scores, axis=2, keepdims=True)
    raised = jnp.exp(scores - row_top)
    return raised / jnp.sum(raised, axis=2, keepdims=True)


def score_grads(weights_full, key_heads, value_heads, attended, grad_heads):
    delta_rows = jnp.sum(grad_heads.astype(jnp.float32) * attended.astype(jnp.float32), axis=2).T
    prob_grad = jnp.einsum(
        "qhe,khe->hqk", grad_heads, value_heads, preferred_element_type=jnp.float32
    )
    score_grad = (weights_full * (prob_grad - delta_rows[:, :, None])).astype(jnp.bfloat16)
    query_grad = (
        jnp.einsum("hqk,khe->qhe", score_grad, key_heads, preferred_element_type=jnp.float32)
        * HEAD ** (-0.5)
    ).astype(jnp.bfloat16)
    return (query_grad, score_grad)


def body(queries, keys, values, segment_ids, out_weight, out_grad):
    tok_rows = queries.shape[1]
    width_all = queries.shape[2]
    head_count = width_all // HEAD
    factor = HEAD ** (-0.5)
    grad_rows = out_grad[0]
    attended_grad = lax.dot_general(
        grad_rows, out_weight, (((1,), (1,)), ((), ())), preferred_element_type=jnp.float32
    ).astype(jnp.bfloat16)
    query_heads = queries[0].reshape(tok_rows, head_count, HEAD)
    grad_heads = attended_grad.reshape(tok_rows, head_count, HEAD)
    query_places = lax.axis_index("seq") * tok_rows + jnp.arange(tok_rows, dtype=jnp.int32)
    key_all, value_all, docs_all = (
        lax.all_gather(keys, "seq", axis=1, tiled=True),
        lax.all_gather(values, "seq", axis=1, tiled=True),
        lax.all_gather(segment_ids, "seq", axis=1, tiled=True),
    )
    key_all = key_all[0].reshape(-1, head_count, HEAD)
    value_all = value_all[0].reshape(-1, head_count, HEAD)
    docs_all = docs_all[0]
    key_places = jnp.arange(docs_all.shape[0], dtype=jnp.int32)
    weights_full = attention_weights(
        query_heads, key_all, query_places, key_places, segment_ids[0], docs_all
    )
    weights_low = weights_full.astype(jnp.bfloat16)
    attended = jnp.einsum(
        "hqk,khe->qhe", weights_low, value_all, preferred_element_type=jnp.float32
    ).astype(jnp.bfloat16)
    query_grad, score_grad = score_grads(weights_full, key_all, value_all, attended, grad_heads)
    key_term = (
        jnp.einsum("hqk,qhe->khe", score_grad, query_heads, preferred_element_type=jnp.float32)
        * factor
    )
    value_term = jnp.einsum(
        "hqk,qhe->khe", weights_low, grad_heads, preferred_element_type=jnp.float32
    )
    summed = lax.psum_scatter(
        jnp.concatenate(
            [
                key_term.reshape(tok_rows * lax.axis_size("seq"), width_all),
                value_term.reshape(tok_rows * lax.axis_size("seq"), width_all),
            ],
            axis=1,
        ),
        "seq",
        scatter_dimension=0,
        tiled=True,
    )
    key_out = summed[:, :width_all].astype(jnp.bfloat16)
    value_out = summed[:, width_all:].astype(jnp.bfloat16)
    attended_flat = attended.reshape(tok_rows, width_all)
    query_out = query_grad.reshape(tok_rows, width_all)
    projected = jnp.dot(attended_flat, out_weight, preferred_element_type=jnp.float32).astype(
        jnp.bfloat16
    )
    shares = lax.psum_scatter(
        lax.dot_general(
            attended_flat, grad_rows, (((0,), (0,)), ((), ())), preferred_element_type=jnp.float32
        ),
        "dp",
        scatter_dimension=0,
        tiled=True,
    )
    weight_grad = lax.psum(shares, "seq").astype(jnp.bfloat16)
    return (projected[None], query_out[None], key_out[None], value_out[None], weight_grad)


def solution(mesh):
    placed = (
        P("dp", "seq", None),
        P("dp", "seq", None),
        P("dp", "seq", None),
        P("dp", "seq"),
        P(),
        P("dp", "seq", None),
    )
    return jax.shard_map(
        body,
        mesh=mesh,
        in_specs=placed,
        out_specs=(
            P("dp", "seq", None),
            P("dp", "seq", None),
            P("dp", "seq", None),
            P("dp", "seq", None),
            P("dp", None),
        ),
        check_vma=False,
    )
```

profile of v0, /device:TPU:1, one launch (start us, length us, event | category | flops | bytes accessed | tf_op | source)
XLA Modules:
  0.0 605.1 jit_solution(7253317289137722357)
XLA Ops:
  7.2 0.0 copy-start
  7.2 0.0 all-gather.3.cloned.1.call-start
  7.2 2.1 copy.21
  9.3 0.0 all-gather.3.cloned.1.call-update
  9.4 0.0 all-gather.5.cloned.1.call-start
  9.4 0.7 all-gather.5.cloned.1.call-update
  10.1 0.0 reduce-scatter.3.cloned.1.call-start
  10.2 1.2 copy.35
  11.4 0.0 copy-done
  11.4 0.0 copy-start.3
  11.4 3.5 convolution_convert_fusion.2
  14.9 0.2 copy.25
  15.1 0.0 copy-done.3
  15.1 8.1 %all_gather.11 = s32[1,1024]{1,0:T(1,128)S(1)} all-gather(s32[1,256]{1,0:T(1,128)S(1)} %copy-done.3), channel_id=1, replica_groups=mesh['dp'=64,'seq'=4] {'seq'}, dimensions={1}, use_global_device_ids=true | all-gather | bytes 5120 | tf_op jit(solution)/shard_map/all_gather | solution.py:50
  23.3 0.3 fusion.11
  23.6 22.6 %all-gather.3.cloned.1.call-done = bf16[1,1024,1024]{1,2,0:T(8,128)(2,1)} async-done(((bf16[1,256,1024]{1,2,0:T(8,128)(2,1)}), bf16[1,1024,1024]{1,2,0:T(8,128)(2,1)}) %all-gather.3.cloned.1.call-update) | async-done | bytes 2097168 | tf_op jit(solution)/shard_map/all_gather | solution.py:48
  46.2 8.1 %fusion.16 = (f32[8,256]{1,0:T(8,128)S(1)}, f32[8,256,1024]{2,1,0:T(8,128)}) fusion(pred[256,1024]{1,0:T(8,128)(4,1)S(1)} %fusion.11, bf16[256,8,128]{0,2,1:T(8,128)(2,1)S(1)} %bitcast.52, bf16[1024,8,128]{0,2,1:T(8,128)(2,1)} %bitcast.63), kind=kOutput, calls=%fused_computation.30 | convolution fusion | flops 545260544 | bytes 11280384 | tf_op jit(solution)/shard_map/sub | solution.py:18
  54.3 5.3 fusion.5
  59.6 21.0 %all-gather.5.cloned.1.call-done = bf16[1,1024,1024]{2,1,0:T(8,128)(2,1)} async-done(((bf16[1,256,1024]{2,1,0:T(8,128)(2,1)}), bf16[1,1024,1024]{2,1,0:T(8,128)(2,1)}) %all-gather.5.cloned.1.call-update) | async-done | bytes 2097168 | tf_op jit(solution)/shard_map/all_gather | solution.py:49
  80.6 4.0 copy.24
  84.5 0.0 copy-start.1
  84.5 4.5 multiply_reduce_fusion
  89.1 0.0 copy-done.1
  89.1 2.7 fusion.17
  91.8 5.3 copy.30
  97.1 5.0 multiply_convert_fusion
  102.2 0.0 copy-start.2
  102.2 3.3 convolution_multiply_fusion
  105.4 0.0 copy-done.2
  105.4 5.4 copy.29
  110.8 7.8 %pad_maximum_fusion = f32[1024,2048]{1,0:T(8,128)} fusion(f32[1024,1024]{1,0:T(8,128)} %copy.30, f32[1024,1024]{1,0:T(8,128)} %copy.29), kind=kLoop, calls=%fused_computation.1 | loop fusion | flops 2097152 | bytes 16777216 | tf_op jit(solution)/shard_map/concatenate | solution.py:72
  118.6 0.0 reduce-scatter.3.cloned.1.call-update
  118.6 0.2 reduce-scatter.5.cloned.1.call-start
  118.8 4.5 fusion.8
  123.3 0.0 reduce-scatter.5.cloned.1.call-update
  123.3 4.4 fusion.7
  127.7 1.0 copy.31
  128.7 4.7 fusion.6
  133.4 67.7 %reduce-scatter.3.cloned.1.call-done = f32[256,2048]{1,0:T(8,128)} async-done(((f32[1024,2048]{1,0:T(8,128)}), f32[256,2048]{1,0:T(8,128)}) %reduce-scatter.3.cloned.1.call-update) | async-done | bytes 2097168 | tf_op jit(solution)/shard_map/reduce_scatter | solution.py:71
  201.1 1.7 convert.4
  202.8 1.0 slice_bitcast_fusion
  203.9 333.0 %reduce-scatter.5.cloned.1.call-done = f32[16,2048]{1,0:T(8,128)} async-done(((f32[1024,2048]{1,0:T(8,128)}), f32[16,2048]{1,0:T(8,128)}) %reduce-scatter.5.cloned.1.call-update) | async-done | bytes 131088 | tf_op jit(solution)/shard_map/reduce_scatter | solution.py:90
  536.9 61.7 %all-reduce.1 = bf16[16,2048]{1,0:T(8,128)(2,1)} all-reduce(f32[16,2048]{1,0:T(8,128)} %reduce-scatter.5.cloned.1.call-done), channel_id=1, replica_groups=mesh['dp'=64,'seq'=4] {'seq'}, use_global_device_ids=true, to_apply=%region_5.6 | all-reduce | flops 32768 | bytes 196608 | tf_op jit(solution)/shard_map/psum | solution.py:98
  (1 shorter events, 0.0 us)
Async XLA Ops:
  7.2 4.3 copy-start
  7.2 39.0 %all-gather.3.cloned.1.call-start = ((), (), s32[]{:S(2)}) async-start(), calls=%async_computation.2 | async-start | bytes 2621440 | tf_op jit(solution)/shard_map/all_gather | solution.py:48
  9.4 71.2 %all-gather.5.cloned.1.call-start = ((), (), s32[]{:S(2)}) async-start(), calls=%async_computation.3 | async-start | bytes 2621440 | tf_op jit(solution)/shard_map/all_gather | solution.py:49
  10.1 191.0 %reduce-scatter.3.cloned.1.call-start = ((), (), s32[]{:S(2)}) async-start(), calls=%async_computation.4 | async-start | bytes 10485760 | tf_op jit(solution)/shard_map/reduce_scatter | solution.py:71
  11.4 3.7 copy-start.3
  84.5 4.6 copy-start.1
  102.2 3.3 copy-start.2
  118.6 418.3 %reduce-scatter.5.cloned.1.call-start = ((), (), s32[]{:S(2)}) async-start(), calls=%async_computation.5 | async-start | bytes 8519680 | tf_op jit(solution)/shard_map/reduce_scatter | solution.py:90
Sparse Core Ops, SparseCore 0:
  10.4 35.7 all-gather.2
  48.0 32.5 all-gather.4
  118.7 82.3 reduce-scatter.2
  203.5 333.3 reduce-scatter.4
where the time goes:
time: 606 us; the launch traced here: 605 us
  waiting for transfers between devices  445 us (73%)
  blocking collectives  69.8 us (12%)
  matrix products  40.6 us (7%)
  local copies, waits for them, and re-layouts  20.3 us (3%)
  other arithmetic  15.1 us (2%)
  between operations  13.9 us (2%)
    reduce_scatter x1, waiting for transfers between devices, body(): lax.psum_scatter(lax.dot_general(attended_flat, grad_rows, (((0,), (0,)),...  333 us
    reduce_scatter x1, waiting for transfers between devices, body(): lax.psum_scatter(jnp.concatenate([key_term.reshape(tok_rows * lax.axis_si...  67.7 us
    psum x1, blocking collectives, body(): weight_grad = lax.psum(shares, 'seq').astype(jnp.bfloat16)  61.7 us
    all_gather x1, waiting for transfers between devices, body(): lax.all_gather(keys, 'seq', axis=1, tiled=True)  22.6 us
    all_gather x1, waiting for transfers between devices, body(): lax.all_gather(values, 'seq', axis=1, tiled=True)  21 us
  transfers between devices with their start and end apart: 4, of which 4 were waited for; matrix products, arithmetic and copies ran while one was open for 6% of the time, Pallas kernels for 0%

commit v1 on v0

v1 whole, which is shorter than its diff:
```python
import jax
import jax.numpy as jnp
from jax import lax
from jax.experimental import pallas as pl
from jax.experimental.pallas import tpu as pltpu
from jax.sharding import PartitionSpec as P

HEAD = 128
PLANES, RING, SIDES = 8, 4, 2
MESH = pl.DeviceIdType.MESH
F32, BF16 = jnp.float32, jnp.bfloat16
LOG2E = 1.4426950408889634


def dot(a, b, ca, cb):
    return lax.dot_general(a, b, (((ca,), (cb,)), ((), ())), preferred_element_type=F32)


def kernel(
    q_hbm, k_hbm, v_hbm, seg_ref, w_hbm, og_hbm,
    proj_out, dq_out, dk_out, dv_out, wg_out,
    q_s, kv, og, w, og2, dgrad, att, seg_own, seg_all, bias,
    dkv_own, dkv_out, dkv_in, part, y1_in, y1_sum, y2_in, z_out, z_in, x_out, x_in, fin, fin_in,
    q_sem, kv_sem, og_sem, w_sem, og2_sem, seg_send, seg_recv, ogs_send, ogs_recv,
    kv1_send, kv1_recv, kv2_send, kv2_recv, dk1_send, dk1_recv, dk2_send, dk2_recv,
    att_send, att_recv, y1_send, y1_recv, y2_send, y2_recv, z_send, z_recv,
    x_send, x_recv, f_send, f_recv,
):
    heads, toks = q_s.shape[0], q_s.shape[1]
    cols = og2.shape[1]
    rows = HEAD // RING
    share = rows // SIDES
    s = lax.axis_index("seq")
    d = lax.axis_index("dp")
    core = s % 2
    lo = s // 2
    z = d // (RING * SIDES)
    y = (d // SIDES) % RING
    hi = d % SIDES
    sib = s + 1 - 2 * core
    flip = y + 1 - 2 * (y % 2)
    mirror = RING - 1 - y
    ya = core * mirror + (1 - core) * flip
    yb = core * flip + (1 - core) * mirror
    yc = (y + 2) % RING

    def place(zz, yy, xx):
        return zz * (RING * SIDES) + yy * SIDES + xx

    def remote(src, dst, send, recv, dp, seq):
        return pltpu.make_async_remote_copy(
            src_ref=src, dst_ref=dst, send_sem=send, recv_sem=recv,
            device_id=(dp, seq), device_id_type=MESH,
        )

    def lanes(h):
        return pl.ds(pl.multiple_of(h * HEAD, HEAD), HEAD)

    def load_head(i, c):
        h = (z + 1 + i) % heads
        pltpu.make_async_copy(k_hbm.at[:, lanes(h)], kv.at[h, 2, 0], kv_sem.at[h]).start()
        pltpu.make_async_copy(v_hbm.at[:, lanes(h)], kv.at[h, 2, 1], kv_sem.at[h]).start()
        return c

    lax.fori_loop(0, heads, load_head, 0)
    og_copy = pltpu.make_async_copy(og_hbm, og, og_sem)
    w_copy = pltpu.make_async_copy(w_hbm, w, w_sem)
    og_copy.start()
    w_copy.start()

    def load_query(i, c):
        pltpu.make_async_copy(q_hbm.at[:, lanes(i)], q_s.at[i], q_sem).start()
        return c

    lax.fori_loop(0, heads, load_query, 0)
    mine = pl.ds(pl.multiple_of(core * cols, cols), cols)
    other = pl.ds(pl.multiple_of((1 - core) * cols, cols), cols)
    og2_copy = pltpu.make_async_copy(og_hbm.at[:, mine], og2.at[pl.ds(0, toks)], og2_sem)
    og2_copy.start()

    barrier = pltpu.get_barrier_semaphore()
    peers = [(d, (s + 1) % 4), (d, (s + 2) % 4), (d, (s + 3) % 4)]
    peers += [(place(z, flip, hi), s), (place(z, mirror, hi), s)]
    peers += [(place((z + i) % PLANES, y, hi), s) for i in range(1, PLANES)]
    if SIDES == 2:
        peers += [(place(z, y, 1 - hi), core), (place(z, y, 1 - hi), 2 + core)]
    for peer in peers:
        pl.semaphore_signal(barrier, inc=1, device_id=peer, device_id_type=MESH)

    seg_own[...] = jnp.broadcast_to(seg_ref[0:1, :].astype(F32), seg_own.shape)
    seg_all[2] = seg_own[...]

    @pl.when(s < 2)
    def _():
        seg_all[0] = jnp.full(seg_own.shape, -1.0, F32)

        def clear(h, c):
            kv[h, 0] = jnp.zeros((2, toks, HEAD), BF16)
            return c

        lax.fori_loop(0, heads, clear, 0)

    @pl.when(s < 1)
    def _():
        seg_all[1] = jnp.full(seg_own.shape, -1.0, F32)

        def clear(h, c):
            kv[h, 1] = jnp.zeros((2, toks, HEAD), BF16)
            return c

        lax.fori_loop(0, heads, clear, 0)

    def wait_head(h, c):
        pltpu.make_async_copy(kv.at[h, 2], kv.at[h, 2], kv_sem.at[h]).wait()
        return c

    lax.fori_loop(0, heads, wait_head, 0)
    pl.semaphore_wait(barrier, len(peers))

    def kv1(h):
        return remote(kv.at[h, 2], kv.at[h, 1], kv1_send.at[h], kv1_recv.at[h], d, (s + 1) % 4)

    def kv2(h):
        return remote(kv.at[h, 2], kv.at[h, 0], kv2_send.at[h], kv2_recv.at[h], d, (s + 2) % 4)

    def kv2_relay(h):
        return remote(kv.at[h, 1], kv.at[h, 0], kv2_send.at[h], kv2_recv.at[h], d, (s + 1) % 4)

    def send_kv(t):
        h = (z + 1 + t) % heads

        @pl.when(s < 3)
        def _():
            kv1(h).start()

        @pl.when(s == 0)
        def _():
            kv2(h).start()

    seg1 = remote(seg_own, seg_all.at[1], seg_send.at[0], seg_recv.at[0], d, (s + 1) % 4)
    seg2 = remote(seg_own, seg_all.at[0], seg_send.at[1], seg_recv.at[1], d, (s + 2) % 4)

    @pl.when(s < 3)
    def _():
        seg1.start()

    @pl.when(s < 2)
    def _():
        seg2.start()

    send_kv(0)
    send_kv(1)
    ogs = remote(
        og_hbm.at[:, other], og2.at[pl.ds(toks, toks)], ogs_send, ogs_recv, d, sib
    )
    ogs.start()

    og_copy.wait()
    w_copy.wait()

    def grad_pair(i, c):
        at = pl.ds(pl.multiple_of(i * 2 * HEAD, 2 * HEAD), 2 * HEAD)
        g = dot(w[at, :], og[...], 1, 1).astype(BF16)
        dgrad[2 * i] = g[:HEAD]
        dgrad[2 * i + 1] = g[HEAD:]
        return c

    lax.fori_loop(0, heads // 2, grad_pair, 0)

    @pl.when(s >= 1)
    def _():
        seg1.wait_recv()

    @pl.when(s >= 2)
    def _():
        seg2.wait_recv()

    down = lax.broadcasted_iota(jnp.int32, (toks, toks), 0)
    across = lax.broadcasted_iota(jnp.int32, (toks, toks), 1)
    row = seg_all[2][0:1, :]
    for j in range(3):
        column = jnp.sum(
            jnp.where(down == across, jnp.broadcast_to(seg_all[j][0:1, :], (toks, toks)), 0.0),
            axis=1, keepdims=True,
        )
        seen = column == row
        if j == 2:
            seen = seen & (down <= across)
        bias[j * toks:(j + 1) * toks, :] = jnp.where(seen, 0.0, -1e30)

    pltpu.make_async_copy(q_s, q_s, q_sem).wait()

    def attend(h):
        q = q_s[h]
        k3 = kv[h, :, 0].reshape(3 * toks, HEAD)
        v3 = kv[h, :, 1].reshape(3 * toks, HEAD)
        g = dgrad[h]
        score = dot(k3, q, 1, 1) * (HEAD ** -0.5 * LOG2E) + bias[...]
        raised = jnp.exp2(score - jnp.max(score, axis=0, keepdims=True))
        prob = raised * (1.0 / jnp.sum(raised, axis=0, keepdims=True))
        low = prob.astype(BF16)
        a = dot(v3, low, 0, 0).astype(BF16)
        att[h, :, 0:toks] = a
        delta = jnp.sum(g.astype(F32) * a.astype(F32), axis=0, keepdims=True)
        change = (prob * (dot(v3, g, 1, 0) - delta)).astype(BF16)
        dq = dot(k3, change, 0, 0) * HEAD ** -0.5
        dq_out[:, lanes(h)] = dq.T.astype(BF16)
        dk = dot(change, q, 1, 0) * HEAD ** -0.5
        dv = dot(low, g, 1, 1)
        for i, term in enumerate((dk, dv)):
            dkv_own[h, i] = term[2 * toks:]
            dkv_out[h, 0, i] = term[toks:2 * toks].astype(BF16)
            dkv_out[h, 1, i] = term[:toks].astype(BF16)

    def att_copy(h):
        return remote(
            att.at[h, :, pl.ds(0, toks)], att.at[h, :, pl.ds(toks, toks)],
            att_send.at[h], att_recv.at[h], d, sib,
        )

    def back1(h):
        return remote(
            dkv_out.at[h, 0], dkv_in.at[0, h], dk1_send.at[h], dk1_recv.at[h], d, (s + 3) % 4
        )

    def back2(h):
        return remote(
            dkv_out.at[h, 1], dkv_in.at[1, h], dk2_send.at[h], dk2_recv.at[h], d,
            (s + 3 - (1 - core)) % 4,
        )

    def y1_copy(h, j):
        block = ya if j == 0 else yc
        return remote(
            part.at[h, pl.ds(pl.multiple_of(block * rows, rows), rows)], y1_in.at[h, j],
            y1_send.at[h, j], y1_recv.at[h, j], place(z, ya, hi), s,
        )

    def y2_copy(h):
        return remote(
            y1_sum.at[h], y2_in.at[h], y2_send.at[h], y2_recv.at[h], place(z, yb, hi), s
        )

    def z_copy(t):
        h = (z + 1 + t) % heads
        slot = heads - 2 - t
        return remote(
            z_out.at[h], z_in.at[slot], z_send.at[slot], z_recv.at[slot], place(h, y, hi), s
        )

    def own(h, block):
        return part[h, pl.ds(pl.multiple_of(block * rows, rows), rows), :].astype(F32)

    def step(t, c):
        @pl.when(t < heads - 2)
        def _():
            h = (z + 1 + t) % heads

            @pl.when(s < 3)
            def _():
                kv1(h).wait_send()

            @pl.when(s == 0)
            def _():
                kv2(h).wait_send()

            send_kv(t + 2)

        @pl.when((t >= 1) & (t <= heads))
        def _():
            h = (z + t) % heads

            @pl.when(s == 2)
            def _():
                back2(h).wait_recv()
                dkv_out[h, 0] = (
                    dkv_out[h, 0].astype(F32) + dkv_in[1, h].astype(F32)
                ).astype(BF16)
                back1(h).start()

            att_copy(h).wait_recv()
            part[h] = dot(att[h], og2[...], 1, 0).astype(BF16)
            y1_copy(h, 0).start()
            y1_copy(h, 1).start()

        @pl.when((t >= 2) & (t <= heads + 1))
        def _():
            h = (z + t - 1) % heads
            y1_copy(h, 0).wait_recv()
            y1_copy(h, 1).wait_recv()
            y1_sum[h] = (own(h, yb) + y1_in[h, 1].astype(F32)).astype(BF16)
            y2_copy(h).start()

        @pl.when(t >= 3)
        def _():
            h = (z + t - 2) % heads
            y2_copy(h).wait_recv()
            z_out[h] = (own(h, y) + y1_in[h, 0].astype(F32) + y2_in[h].astype(F32)).astype(BF16)

            @pl.when(t < heads + 2)
            def _():
                z_copy(t - 3).start()

        @pl.when(t < heads)
        def _():
            h = (z + 1 + t) % heads

            @pl.when(s >= 1)
            def _():
                kv1(h).wait_recv()

            @pl.when(s == 2)
            def _():
                kv2_relay(h).start()

            @pl.when(s >= 2)
            def _():
                kv2(h).wait_recv()

            attend(h)
            att_copy(h).start()

            @pl.when((s == 1) | (s == 3))
            def _():
                back1(h).start()

            @pl.when(s >= 2)
            def _():
                back2(h).start()

        @pl.when(t == heads)
        def _():
            flat = att[:, :, 0:toks].reshape(heads * HEAD, toks).T

            def project(i, cc):
                at = pl.ds(pl.multiple_of(i * 512, 512), 512)
                proj_out[:, at] = dot(flat, w[:, at], 1, 0).astype(BF16)
                return cc

            width = proj_out.shape[1]
            if width >= 512:
                lax.fori_loop(0, width // 512, project, 0)
            else:
                proj_out[...] = dot(flat, w[...], 1, 0).astype(BF16)

        return c

    og2_copy.wait()
    ogs.wait_recv()
    lax.fori_loop(0, heads + 3, step, 0)

    total = z_out[z].astype(F32)
    for slot in range(PLANES - 1):
        z_copy(heads - 2 - slot).wait_recv()
        total = total + z_in[slot].astype(F32)
    x_out[...] = total
    x_copies = []
    targets = [(d, (1 - lo) * 2 + core, hi)]
    if SIDES == 2:
        targets += [(place(z, y, 1 - hi), core, 1 - hi), (place(z, y, 1 - hi), 2 + core, 1 - hi)]
    for i, (dp, seq, part_of) in enumerate(targets):
        slot = i if i == 0 else 1 + (i - 1 + lo) % 2
        copy = remote(
            x_out.at[pl.ds(pl.multiple_of(part_of * share, share), share)], x_in.at[slot],
            x_send.at[i], x_recv.at[slot], dp, seq,
        )
        copy.start()
        x_copies.append(copy)

    def finish(h, c):
        @pl.when(s < 3)
        def _():
            back1(h).wait_recv()

        @pl.when(s == 0)
        def _():
            back2(h).wait_recv()

        for i, out in enumerate((dk_out, dv_out)):
            @pl.when(s == 3)
            def _():
                out[:, lanes(h)] = dkv_own[h, i].astype(BF16)

            @pl.when((s == 1) | (s == 2))
            def _():
                out[:, lanes(h)] = (dkv_own[h, i] + dkv_in[0, h, i].astype(F32)).astype(BF16)

            @pl.when(s == 0)
            def _():
                out[:, lanes(h)] = (
                    dkv_own[h, i] + dkv_in[0, h, i].astype(F32) + dkv_in[1, h, i].astype(F32)
                ).astype(BF16)

        return c

    lax.fori_loop(0, heads, finish, 0)

    result = x_out[pl.ds(pl.multiple_of(hi * share, share), share), :]
    for slot in range(len(targets)):
        pltpu.make_async_copy(x_in.at[slot], x_in.at[slot], x_recv.at[slot]).wait()
        result = result + x_in[slot]
    fin[...] = result.astype(BF16)
    last = remote(fin, fin_in, f_send, f_recv, d, sib)
    last.start()
    wg_out[:, mine] = fin[...]

    def drain(h, c):
        @pl.when((s < 3) & (h >= heads - 2))
        def _():
            kv1((z + 1 + h) % heads).wait_send()

        @pl.when((s == 0) & (h >= heads - 2))
        def _():
            kv2((z + 1 + h) % heads).wait_send()

        @pl.when(s == 2)
        def _():
            kv2_relay(h).wait_send()

        @pl.when(s >= 1)
        def _():
            back1(h).wait_send()

        @pl.when(s >= 2)
        def _():
            back2(h).wait_send()

        att_copy(h).wait_send()
        y1_copy(h, 0).wait_send()
        y1_copy(h, 1).wait_send()
        y2_copy(h).wait_send()

        @pl.when(h < heads - 1)
        def _():
            z_copy(h).wait_send()

        return c

    lax.fori_loop(0, heads, drain, 0)
    ogs.wait_send()
    for copy in x_copies:
        copy.wait_send()

    @pl.when(s < 3)
    def _():
        seg1.wait_send()

    @pl.when(s < 2)
    def _():
        seg2.wait_send()

    last.wait()
    wg_out[:, other] = fin_in[...]


def body(queries, keys, values, segment_ids, out_weight, out_grad):
    toks, hd = queries.shape[1:]
    width = out_grad.shape[2]
    heads = hd // HEAD
    cols = width // 2
    rows = HEAD // RING
    share = rows // SIDES
    sem = pltpu.SemaphoreType.DMA
    any_space = pl.BlockSpec(memory_space=pl.ANY)
    in_vmem = pl.BlockSpec(memory_space=pltpu.VMEM)
    outs = pl.pallas_call(
        kernel,
        out_shape=(
            jax.ShapeDtypeStruct((toks, width), BF16),
            jax.ShapeDtypeStruct((toks, hd), BF16),
            jax.ShapeDtypeStruct((toks, hd), BF16),
            jax.ShapeDtypeStruct((toks, hd), BF16),
            jax.ShapeDtypeStruct((share, width), BF16),
        ),
        in_specs=[any_space, any_space, any_space, in_vmem, any_space, any_space],
        out_specs=(in_vmem,) * 5,
        scratch_shapes=[
            pltpu.VMEM((heads, toks, HEAD), BF16),
            pltpu.VMEM((heads, 3, 2, toks, HEAD), BF16),
            pltpu.VMEM((toks, width), BF16),
            pltpu.VMEM((hd, width), BF16),
            pltpu.VMEM((2 * toks, cols), BF16),
            pltpu.VMEM((heads, HEAD, toks), BF16),
            pltpu.VMEM((heads, HEAD, 2 * toks), BF16),
            pltpu.VMEM((8, toks), F32),
            pltpu.VMEM((3, 8, toks), F32),
            pltpu.VMEM((3 * toks, toks), F32),
            pltpu.VMEM((heads, 2, toks, HEAD), F32),
            pltpu.VMEM((heads, 2, 2, toks, HEAD), BF16),
            pltpu.VMEM((2, heads, 2, toks, HEAD), BF16),
            pltpu.VMEM((heads, HEAD, cols), BF16),
            pltpu.VMEM((heads, 2, rows, cols), BF16),
            pltpu.VMEM((heads, rows, cols), BF16),
            pltpu.VMEM((heads, rows, cols), BF16),
            pltpu.VMEM((heads, rows, cols), BF16),
            pltpu.VMEM((PLANES - 1, rows, cols), BF16),
            pltpu.VMEM((rows, cols), F32),
            pltpu.VMEM((3, share, cols), F32),
            pltpu.VMEM((share, cols), BF16),
            pltpu.VMEM((share, cols), BF16),
            sem, sem((heads,)), sem, sem, sem, sem((2,)), sem((2,)), sem, sem,
            sem((heads,)), sem((heads,)), sem((heads,)), sem((heads,)),
            sem((heads,)), sem((heads,)), sem((heads,)), sem((heads,)),
            sem((heads,)), sem((heads,)), sem((heads, 2)), sem((heads, 2)),
            sem((heads,)), sem((heads,)), sem((PLANES - 1,)), sem((PLANES - 1,)),
            sem((3,)), sem((3,)), sem, sem,
        ],
        compiler_params=pltpu.CompilerParams(
            collective_id=0, has_side_effects=True, vmem_limit_bytes=56 << 20
        ),
        cost_estimate=pl.CostEstimate(
            flops=8 << 30, bytes_accessed=10 << 20, transcendentals=2 << 20
        ),
    )(queries[0], keys[0], values[0], segment_ids, out_weight, out_grad[0])
    return tuple(out[None] for out in outs[:4]) + (outs[4],)


def solution(mesh):
    placed = (
        P("dp", "seq", None),
        P("dp", "seq", None),
        P("dp", "seq", None),
        P("dp", "seq"),
        P(),
        P("dp", "seq", None),
    )
    return jax.shard_map(
        body,
        mesh=mesh,
        in_specs=placed,
        out_specs=placed[:1] * 4 + (P("dp", None),),
        check_vma=False,
    )
```

time: 606 us -> 73.1 us (0.12)
  waiting for transfers between devices: 445 us -> 0 us
  blocking collectives: 69.8 us -> 0 us
  Pallas kernels: 0 us -> 64.7 us
  matrix products: 40.6 us -> 0 us
  other arithmetic: 15.1 us -> 0 us
  between operations: 13.9 us -> 0.66 us
  local copies, waits for them, and re-layouts: 20.3 us -> 7.53 us
    reduce_scatter x2 -> x0, waiting for transfers between devices: 401 us -> none  [the longest x1 333 us: body(): lax.psum_scatter(lax.dot_general(attended_flat, grad_rows, (((0,), (0,)),...]
    pallas_call x0 -> x1, Pallas kernels: none -> 64.7 us  [body(): pl.pallas_call(kernel, out_shape=(jax.ShapeDtypeStruct((toks, width), BF1...]
    psum x1 -> x0, blocking collectives: 61.7 us -> none  [body(): weight_grad = lax.psum(shares, 'seq').astype(jnp.bfloat16)]
    all_gather x2 -> x0, waiting for transfers between devices: 43.6 us -> none  [the longest x1 22.6 us: body(): lax.all_gather(keys, 'seq', axis=1, tiled=True)]
    dot_general x8 -> x0, matrix products: 32.5 us -> none  [the longest x1 5.02 us: score_grads(): jnp.einsum('qhe,khe->hqk', grad_heads, value_heads, preferred_element_typ...]
    reshape x2 -> x0, local copies, waits for them, and re-layouts: 10.7 us -> none  [the longest x1 5.36 us: body(): key_term.reshape(tok_rows * lax.axis_size('seq'), width_all)]
    all_gather x1 -> x0, blocking collectives: 8.12 us -> none  [body(): lax.all_gather(segment_ids, 'seq', axis=1, tiled=True)]
    sub x1 -> x0, matrix products: 8.09 us -> none  [attention_weights(): raised = jnp.exp(scores - row_top)]
  transfers between devices with their start and end apart: 4 -> 0, of which waited for: 4 -> 0; matrix products, arithmetic and copies ran while one was open for 6% -> 0% of each run, Pallas kernels for 0% -> 0%
where the time goes in v1:
time: 73.1 us; the launch traced here: 72.9 us
  Pallas kernels  64.7 us (89%)
  local copies, waits for them, and re-layouts  7.53 us (10%)
    pallas_call x1, Pallas kernels, body(): pl.pallas_call(kernel, out_shape=(jax.ShapeDtypeStruct((toks, width), BF1...  64.7 us
    unnamed x9, local copies, waits for them, and re-layouts  7.53 us

profile of v1, /device:TPU:1, one launch (start us, length us, event | category | flops | bytes accessed | tf_op | source)
XLA Modules:
  0.0 72.9 jit_solution(16518357931991277929)
XLA Ops:
  0.6 64.7 %shard_map.101 = (bf16[256,2048]{1,0:T(8,128)(2,1)}, bf16[256,1024]{1,0:T(8,128)(2,1)}, bf16[256,1024]{1,0:T(8,128)(2,1)}, bf16[256,1024]{1,0:T(8,128)(2,1)}, bf16[16,2048]{1,0:T(8,128)(2,1)}) custom-call(bf16[256,1024]{1,0:T(8,128)(2,1)} %bitcast.13, bf16[256,1024]{1,0:T(8,128)(2,1)} %bitcast.14, bf16[256,1024]{1,0:T(8,128)(2,1)} %bitcast.15, ...), custom_call_target="tpu_custom_call" | custom-call | flops 8589934592 | bytes 10485760 | tf_op jit(solution)/shard_map/pallas_call | solution.py:466
  65.4 0.0 copy-start
  65.4 0.0 copy-start.1
  65.4 2.4 %copy.16 = bf16[1,256,2048]{2,1,0:T(8,128)(2,1)} copy(bf16[1,256,2048]{2,1,0:T(8,128)(2,1)} %bitcast.8) | data formatting | bytes 2097152
  67.8 1.9 %copy.17 = bf16[1,256,1024]{2,1,0:T(8,128)(2,1)} copy(bf16[1,256,1024]{2,1,0:T(8,128)(2,1)} %bitcast.11) | data formatting | bytes 1048576
  69.6 1.9 %copy.18 = bf16[1,256,1024]{2,1,0:T(8,128)(2,1)} copy(bf16[1,256,1024]{2,1,0:T(8,128)(2,1)} %bitcast.10) | data formatting | bytes 1048576
  71.5 0.0 copy-done
  71.5 0.8 %copy.19 = bf16[1,256,1024]{2,1,0:T(8,128)(2,1)} copy(bf16[1,256,1024]{2,1,0:T(8,128)(2,1)S(1)} %bitcast.9) | data formatting | bytes 1048576
  72.3 0.0 copy-done.1
  72.3 0.6 copy.20
Async XLA Ops:
  65.4 6.1 %copy-start = (bf16[256,1024]{1,0:T(8,128)(2,1)S(1)}, bf16[256,1024]{1,0:T(8,128)(2,1)}, u32[]{:S(2)}) copy-start(bf16[256,1024]{1,0:T(8,128)(2,1)} %get-tuple-element.13) | copy-start | bytes 1572868
  65.4 6.9 %copy-start.1 = (bf16[16,2048]{1,0:T(8,128)(2,1)S(1)}, bf16[16,2048]{1,0:T(8,128)(2,1)}, u32[]{:S(2)}) copy-start(bf16[16,2048]{1,0:T(8,128)(2,1)} %get-tuple-element.24) | copy-start | bytes 196612

commit v2 on v1

--- a/solution.py
+++ b/solution.py
@@ -7,6 +7,7 @@
 
 HEAD = 128
 PLANES, RING, SIDES = 8, 4, 2
+AHEAD = 2
 MESH = pl.DeviceIdType.MESH
 F32, BF16 = jnp.float32, jnp.bfloat16
 LOG2E = 1.4426950408889634
@@ -56,8 +57,16 @@
     def lanes(h):
         return pl.ds(pl.multiple_of(h * HEAD, HEAD), HEAD)
 
+    def apart(t):
+        even = heads // 2 + t // 2
+        odd = (heads - 1 - t) // 2
+        return even + (t % 2) * (odd - even)
+
+    def order(t):
+        return (z + apart(t)) % heads
+
     def load_head(i, c):
-        h = (z + 1 + i) % heads
+        h = order(i)
         pltpu.make_async_copy(k_hbm.at[:, lanes(h)], kv.at[h, 2, 0], kv_sem.at[h]).start()
         pltpu.make_async_copy(v_hbm.at[:, lanes(h)], kv.at[h, 2, 1], kv_sem.at[h]).start()
         return c
@@ -127,7 +136,7 @@
         return remote(kv.at[h, 1], kv.at[h, 0], kv2_send.at[h], kv2_recv.at[h], d, (s + 1) % 4)
 
     def send_kv(t):
-        h = (z + 1 + t) % heads
+        h = order(t)
 
         @pl.when(s < 3)
         def _():
@@ -149,13 +158,11 @@
         seg2.start()
 
     send_kv(0)
-    send_kv(1)
+    og_copy.wait()
     ogs = remote(
-        og_hbm.at[:, other], og2.at[pl.ds(toks, toks)], ogs_send, ogs_recv, d, sib
+        og.at[:, other], og2.at[pl.ds(toks, toks)], ogs_send, ogs_recv, d, sib
     )
     ogs.start()
-
-    og_copy.wait()
     w_copy.wait()
 
     def grad_pair(i, c):
@@ -166,6 +173,8 @@
         return c
 
     lax.fori_loop(0, heads // 2, grad_pair, 0)
+    for t in range(1, AHEAD):
+        send_kv(t)
 
     @pl.when(s >= 1)
     def _():
@@ -201,6 +210,7 @@
         low = prob.astype(BF16)
         a = dot(v3, low, 0, 0).astype(BF16)
         att[h, :, 0:toks] = a
+        att_copy(h).start()
         delta = jnp.sum(g.astype(F32) * a.astype(F32), axis=0, keepdims=True)
         change = (prob * (dot(v3, g, 1, 0) - delta)).astype(BF16)
         dq = dot(k3, change, 0, 0) * HEAD ** -0.5
@@ -242,8 +252,8 @@
         )
 
     def z_copy(t):
-        h = (z + 1 + t) % heads
-        slot = heads - 2 - t
+        h = order(t)
+        slot = heads - 1 - apart(t)
         return remote(
             z_out.at[h], z_in.at[slot], z_send.at[slot], z_recv.at[slot], place(h, y, hi), s
         )
@@ -252,81 +262,63 @@
         return part[h, pl.ds(pl.multiple_of(block * rows, rows), rows), :].astype(F32)
 
     def step(t, c):
-        @pl.when(t < heads - 2)
-        def _():
-            h = (z + 1 + t) % heads
-
-            @pl.when(s < 3)
-            def _():
-                kv1(h).wait_send()
-
-            @pl.when(s == 0)
-            def _():
-                kv2(h).wait_send()
-
-            send_kv(t + 2)
+        @pl.when((t < heads) & (s >= 1))
+        def _():
+            h = order(t)
+            kv1(h).wait_recv()
+
+            @pl.when(s == 2)
+            def _():
+                kv2_relay(h).start()
+
+        @pl.when(t < heads)
+        def _():
+            h = order(t)
+
+            @pl.when(s >= 2)
+            def _():
+                kv2(h).wait_recv()
+
+            attend(h)
+
+            @pl.when((s == 1) | (s == 3))
+            def _():
+                back1(h).start()
+
+            @pl.when(s >= 2)
+            def _():
+                back2(h).start()
 
         @pl.when((t >= 1) & (t <= heads))
         def _():
-            h = (z + t) % heads
-
-            @pl.when(s == 2)
-            def _():
-                back2(h).wait_recv()
-                dkv_out[h, 0] = (
-                    dkv_out[h, 0].astype(F32) + dkv_in[1, h].astype(F32)
-                ).astype(BF16)
-                back1(h).start()
-
+            h = order(t - 1)
             att_copy(h).wait_recv()
             part[h] = dot(att[h], og2[...], 1, 0).astype(BF16)
             y1_copy(h, 0).start()
             y1_copy(h, 1).start()
 
-        @pl.when((t >= 2) & (t <= heads + 1))
-        def _():
-            h = (z + t - 1) % heads
-            y1_copy(h, 0).wait_recv()
-            y1_copy(h, 1).wait_recv()
-            y1_sum[h] = (own(h, yb) + y1_in[h, 1].astype(F32)).astype(BF16)
-            y2_copy(h).start()
-
-        @pl.when(t >= 3)
-        def _():
-            h = (z + t - 2) % heads
-            y2_copy(h).wait_recv()
-            z_out[h] = (own(h, y) + y1_in[h, 0].astype(F32) + y2_in[h].astype(F32)).astype(BF16)
-
-            @pl.when(t < heads + 2)
-            def _():
-                z_copy(t - 3).start()
-
-        @pl.when(t < heads)
-        def _():
-            h = (z + 1 + t) % heads
-
-            @pl.when(s >= 1)
-            def _():
-                kv1(h).wait_recv()
-
-            @pl.when(s == 2)
-            def _():
-                kv2_relay(h).start()
-
-            @pl.when(s >= 2)
-            def _():
-                kv2(h).wait_recv()
-
-            attend(h)
-            att_copy(h).start()
-
-            @pl.when((s == 1) | (s == 3))
-            def _():
-                back1(h).start()
-
-            @pl.when(s >= 2)
-            def _():
-                back2(h).start()
+        @pl.when((s == 2) & (t >= 1) & (t <= heads))
+        def _():
+            h = order(t - 1)
+            back2(h).wait_recv()
+            dkv_out[h, 0] = (
+                dkv_out[h, 0].astype(F32) + dkv_in[1, h].astype(F32)
+            ).astype(BF16)
+            back1(h).start()
+
+        @pl.when(t < heads - AHEAD)
+        def _():
+            h = order(t)
+
+            @pl.when(s < 3)
+            def _():
+                kv1(h).wait_send()
+
+            @pl.when(s == 0)
+            def _():
+                kv2(h).wait_send()
+
+            send_kv(t + AHEAD)
 
         @pl.when(t == heads)
         def _():
@@ -343,17 +335,36 @@
             else:
                 proj_out[...] = dot(flat, w[...], 1, 0).astype(BF16)
 
+        @pl.when((t >= 3) & (t <= heads + 2))
+        def _():
+            h = order(t - 3)
+            y1_copy(h, 0).wait_recv()
+            y1_copy(h, 1).wait_recv()
+            y1_sum[h] = (own(h, yb) + y1_in[h, 1].astype(F32)).astype(BF16)
+            y2_copy(h).start()
+
+        @pl.when(t >= 5)
+        def _():
+            h = order(t - 5)
+            y2_copy(h).wait_recv()
+            z_out[h] = (own(h, y) + y1_in[h, 0].astype(F32) + y2_in[h].astype(F32)).astype(BF16)
+
+            @pl.when(t < heads + 4)
+            def _():
+                z_copy(t - 5).start()
+
         return c
 
     og2_copy.wait()
     ogs.wait_recv()
-    lax.fori_loop(0, heads + 3, step, 0)
+    lax.fori_loop(0, heads + 5, step, 0)
 
     total = z_out[z].astype(F32)
+    for t in range(PLANES - 1):
+        z_copy(t).wait_recv()
     for slot in range(PLANES - 1):
-        z_copy(heads - 2 - slot).wait_recv()
         total = total + z_in[slot].astype(F32)
-    x_out[...] = total
+    x_out[...] = total.astype(BF16)
     x_copies = []
     targets = [(d, (1 - lo) * 2 + core, hi)]
     if SIDES == 2:
@@ -395,23 +406,23 @@
 
     lax.fori_loop(0, heads, finish, 0)
 
-    result = x_out[pl.ds(pl.multiple_of(hi * share, share), share), :]
+    result = x_out[pl.ds(pl.multiple_of(hi * share, share), share), :].astype(F32)
     for slot in range(len(targets)):
         pltpu.make_async_copy(x_in.at[slot], x_in.at[slot], x_recv.at[slot]).wait()
-        result = result + x_in[slot]
+        result = result + x_in[slot].astype(F32)
     fin[...] = result.astype(BF16)
     last = remote(fin, fin_in, f_send, f_recv, d, sib)
     last.start()
     wg_out[:, mine] = fin[...]
 
     def drain(h, c):
-        @pl.when((s < 3) & (h >= heads - 2))
-        def _():
-            kv1((z + 1 + h) % heads).wait_send()
-
-        @pl.when((s == 0) & (h >= heads - 2))
-        def _():
-            kv2((z + 1 + h) % heads).wait_send()
+        @pl.when((s < 3) & (h >= heads - AHEAD))
+        def _():
+            kv1(order(h)).wait_send()
+
+        @pl.when((s == 0) & (h >= heads - AHEAD))
+        def _():
+            kv2(order(h)).wait_send()
 
         @pl.when(s == 2)
         def _():
@@ -451,6 +462,18 @@
 
     last.wait()
     wg_out[:, other] = fin_in[...]
+
+
+def settle(*refs):
+    count = len(refs) // 2
+    copies = [
+        pltpu.make_async_copy(src, dst, refs[-1].at[i])
+        for i, (src, dst) in enumerate(zip(refs[:count], refs[count:-1]))
+    ]
+    for copy in copies:
+        copy.start()
+    for copy in copies:
+        copy.wait()
 
 
 def body(queries, keys, values, segment_ids, out_weight, out_grad):
@@ -463,16 +486,21 @@
     sem = pltpu.SemaphoreType.DMA
     any_space = pl.BlockSpec(memory_space=pl.ANY)
     in_vmem = pl.BlockSpec(memory_space=pltpu.VMEM)
+    in_hbm = pl.BlockSpec(memory_space=pltpu.HBM)
+
+    def stay(x):
+        return pltpu.with_memory_space_constraint(x, pltpu.HBM)
+
     outs = pl.pallas_call(
         kernel,
         out_shape=(
-            jax.ShapeDtypeStruct((toks, width), BF16),
-            jax.ShapeDtypeStruct((toks, hd), BF16),
-            jax.ShapeDtypeStruct((toks, hd), BF16),
-            jax.ShapeDtypeStruct((toks, hd), BF16),
-            jax.ShapeDtypeStruct((share, width), BF16),
+            pltpu.VMEM((toks, width), BF16),
+            pltpu.VMEM((toks, hd), BF16),
+            pltpu.VMEM((toks, hd), BF16),
+            pltpu.VMEM((toks, hd), BF16),
+            pltpu.VMEM((share, width), BF16),
         ),
-        in_specs=[any_space, any_space, any_space, in_vmem, any_space, any_space],
+        in_specs=[in_hbm, in_hbm, in_hbm, in_vmem, in_hbm, in_hbm],
         out_specs=(in_vmem,) * 5,
         scratch_shapes=[
             pltpu.VMEM((heads, toks, HEAD), BF16),
@@ -494,8 +522,8 @@
             pltpu.VMEM((heads, rows, cols), BF16),
             pltpu.VMEM((heads, rows, cols), BF16),
             pltpu.VMEM((PLANES - 1, rows, cols), BF16),
-            pltpu.VMEM((rows, cols), F32),
-            pltpu.VMEM((3, share, cols), F32),
+            pltpu.VMEM((rows, cols), BF16),
+            pltpu.VMEM((3, share, cols), BF16),
             pltpu.VMEM((share, cols), BF16),
             pltpu.VMEM((share, cols), BF16),
             sem, sem((heads,)), sem, sem, sem, sem((2,)), sem((2,)), sem, sem,
@@ -506,12 +534,23 @@
             sem((3,)), sem((3,)), sem, sem,
         ],
         compiler_params=pltpu.CompilerParams(
-            collective_id=0, has_side_effects=True, vmem_limit_bytes=56 << 20
+            collective_id=0, has_side_effects=True, vmem_limit_bytes=54 << 20
         ),
         cost_estimate=pl.CostEstimate(
             flops=8 << 30, bytes_accessed=10 << 20, transcendentals=2 << 20
         ),
-    )(queries[0], keys[0], values[0], segment_ids, out_weight, out_grad[0])
+    )(
+        stay(queries[0]), stay(keys[0]), stay(values[0]), segment_ids, stay(out_weight),
+        stay(out_grad[0]),
+    )
+    outs = pl.pallas_call(
+        settle,
+        out_shape=tuple(jax.ShapeDtypeStruct(out.shape, out.dtype) for out in outs),
+        in_specs=[in_vmem] * 5,
+        out_specs=(any_space,) * 5,
+        scratch_shapes=[sem((5,))],
+        compiler_params=pltpu.CompilerParams(vmem_limit_bytes=4 << 20),
+    )(*[pltpu.with_memory_space_constraint(out, pltpu.VMEM) for out in outs])
     return tuple(out[None] for out in outs[:4]) + (outs[4],)
 
 

time: 73.1 us -> 57.8 us (0.79)
  Pallas kernels: 64.7 us -> 57.1 us
  local copies, waits for them, and re-layouts: 7.53 us -> 0 us
    pallas_call x1 -> x2, Pallas kernels: 64.7 us -> 57.1 us  [the longest x1 55.5 us: body(): pl.pallas_call(kernel, out_shape=(pltpu.VMEM((toks, width), BF16), pltpu....]
    unnamed x9 -> x0, local copies, waits for them, and re-layouts: 7.53 us -> none
where the time goes in v2:
time: 57.8 us; the launch traced here: 57.7 us
  Pallas kernels  57.1 us (99%)
  between operations  0.64 us (1%)
    pallas_call x1, Pallas kernels, body(): pl.pallas_call(kernel, out_shape=(pltpu.VMEM((toks, width), BF16), pltpu....  55.5 us
    pallas_call x1, Pallas kernels, body(): pl.pallas_call(settle, out_shape=tuple((jax.ShapeDtypeStruct(out.shape, o...  1.54 us

profile of v2, /device:TPU:1, one launch (start us, length us, event | category | flops | bytes accessed | tf_op | source)
XLA Modules:
  0.0 57.7 jit_solution(10615400851936198642)
XLA Ops:
  0.6 55.5 %shard_map.101 = (bf16[256,2048]{1,0:T(8,128)(2,1)S(1)}, bf16[256,1024]{1,0:T(8,128)(2,1)S(1)}, bf16[256,1024]{1,0:T(8,128)(2,1)S(1)}, bf16[256,1024]{1,0:T(8,128)(2,1)S(1)}, bf16[16,2048]{1,0:T(8,128)(2,1)S(1)}) custom-call(bf16[256,1024]{1,0:T(8,128)(2,1)} %bitcast.10, bf16[256,1024]{1,0:T(8,128)(2,1)} %bitcast.11, bf16[256,1024]{1,0:T(8,128)(2,1)} %bitcast.12, ...), custom_call_target="tpu_custom_call" | custom-call | flops 8589934592 | bytes 10485760 | tf_op jit(solution)/shard_map/pallas_call | solution.py:494
  56.2 1.5 %shard_map.102 = (bf16[256,2048]{1,0:T(8,128)(2,1)}, bf16[256,1024]{1,0:T(8,128)(2,1)}, bf16[256,1024]{1,0:T(8,128)(2,1)}, bf16[256,1024]{1,0:T(8,128)(2,1)}, bf16[16,2048]{1,0:T(8,128)(2,1)}) custom-call(bf16[256,2048]{1,0:T(8,128)(2,1)S(1)} %get-tuple-element.15.refs_0_, bf16[256,1024]{1,0:T(8,128)(2,1)S(1)} %get-tuple-element.16.refs_1_, ...), custom_call_target="tpu_custom_call" | custom-call | tf_op jit(solution)/shard_map/pallas_call | solution.py:546

commit v3 on v2

--- a/solution.py
+++ b/solution.py
@@ -8,6 +8,7 @@
 HEAD = 128
 PLANES, RING, SIDES = 8, 4, 2
 AHEAD = 2
+LAG = 3
 MESH = pl.DeviceIdType.MESH
 F32, BF16 = jnp.float32, jnp.bfloat16
 LOG2E = 1.4426950408889634
@@ -21,10 +22,10 @@
     q_hbm, k_hbm, v_hbm, seg_ref, w_hbm, og_hbm,
     proj_out, dq_out, dk_out, dv_out, wg_out,
     q_s, kv, og, w, og2, dgrad, att, seg_own, seg_all, bias,
-    dkv_own, dkv_out, dkv_in, part, y1_in, y1_sum, y2_in, z_out, z_in, x_out, x_in, fin, fin_in,
+    dkv_own, dkv_out, dkv_in, part, y_in, z_out, z_in, x_out, x_in, fin, fin_in,
     q_sem, kv_sem, og_sem, w_sem, og2_sem, seg_send, seg_recv, ogs_send, ogs_recv,
     kv1_send, kv1_recv, kv2_send, kv2_recv, dk1_send, dk1_recv, dk2_send, dk2_recv,
-    att_send, att_recv, y1_send, y1_recv, y2_send, y2_recv, z_send, z_recv,
+    att_send, att_recv, y_send, y_recv, z_send, z_recv,
     x_send, x_recv, f_send, f_recv,
 ):
     heads, toks = q_s.shape[0], q_s.shape[1]
@@ -39,12 +40,6 @@
     y = (d // SIDES) % RING
     hi = d % SIDES
     sib = s + 1 - 2 * core
-    flip = y + 1 - 2 * (y % 2)
-    mirror = RING - 1 - y
-    ya = core * mirror + (1 - core) * flip
-    yb = core * flip + (1 - core) * mirror
-    yc = (y + 2) % RING
-
     def place(zz, yy, xx):
         return zz * (RING * SIDES) + yy * SIDES + xx
 
@@ -64,6 +59,15 @@
 
     def order(t):
         return (z + apart(t)) % heads
+
+    barrier = pltpu.get_barrier_semaphore()
+    peers = [(d, (s + 1) % 4), (d, (s + 2) % 4), (d, (s + 3) % 4)]
+    peers += [(place(z, (y + i) % RING, hi), s) for i in range(1, RING)]
+    peers += [(place((z + i) % PLANES, y, hi), s) for i in range(1, PLANES)]
+    if SIDES == 2:
+        peers += [(place(z, y, 1 - hi), core), (place(z, y, 1 - hi), 2 + core)]
+    for peer in peers:
+        pl.semaphore_signal(barrier, inc=1, device_id=peer, device_id_type=MESH)
 
     def load_head(i, c):
         h = order(i)
@@ -87,15 +91,6 @@
     og2_copy = pltpu.make_async_copy(og_hbm.at[:, mine], og2.at[pl.ds(0, toks)], og2_sem)
     og2_copy.start()
 
-    barrier = pltpu.get_barrier_semaphore()
-    peers = [(d, (s + 1) % 4), (d, (s + 2) % 4), (d, (s + 3) % 4)]
-    peers += [(place(z, flip, hi), s), (place(z, mirror, hi), s)]
-    peers += [(place((z + i) % PLANES, y, hi), s) for i in range(1, PLANES)]
-    if SIDES == 2:
-        peers += [(place(z, y, 1 - hi), core), (place(z, y, 1 - hi), 2 + core)]
-    for peer in peers:
-        pl.semaphore_signal(barrier, inc=1, device_id=peer, device_id_type=MESH)
-
     seg_own[...] = jnp.broadcast_to(seg_ref[0:1, :].astype(F32), seg_own.shape)
     seg_all[2] = seg_own[...]
 
@@ -135,17 +130,18 @@
     def kv2_relay(h):
         return remote(kv.at[h, 1], kv.at[h, 0], kv2_send.at[h], kv2_recv.at[h], d, (s + 1) % 4)
 
-    def send_kv(t):
-        h = order(t)
-
+    def send_near(t):
         @pl.when(s < 3)
         def _():
-            kv1(h).start()
-
+            kv1(order(t)).start()
+
+    def send_far(t):
         @pl.when(s == 0)
         def _():
-            kv2(h).start()
-
+            kv2(order(t)).start()
+
+    send_near(0)
+    send_far(0)
     seg1 = remote(seg_own, seg_all.at[1], seg_send.at[0], seg_recv.at[0], d, (s + 1) % 4)
     seg2 = remote(seg_own, seg_all.at[0], seg_send.at[1], seg_recv.at[1], d, (s + 2) % 4)
 
@@ -157,7 +153,6 @@
     def _():
         seg2.start()
 
-    send_kv(0)
     og_copy.wait()
     ogs = remote(
         og.at[:, other], og2.at[pl.ds(toks, toks)], ogs_send, ogs_recv, d, sib
@@ -174,7 +169,8 @@
 
     lax.fori_loop(0, heads // 2, grad_pair, 0)
     for t in range(1, AHEAD):
-        send_kv(t)
+        send_near(t)
+        send_far(t)
 
     @pl.when(s >= 1)
     def _():
@@ -239,16 +235,11 @@
             (s + 3 - (1 - core)) % 4,
         )
 
-    def y1_copy(h, j):
-        block = ya if j == 0 else yc
+    def y_copy(h, j):
+        to = (y + 1 + j) % RING
         return remote(
-            part.at[h, pl.ds(pl.multiple_of(block * rows, rows), rows)], y1_in.at[h, j],
-            y1_send.at[h, j], y1_recv.at[h, j], place(z, ya, hi), s,
-        )
-
-    def y2_copy(h):
-        return remote(
-            y1_sum.at[h], y2_in.at[h], y2_send.at[h], y2_recv.at[h], place(z, yb, hi), s
+            part.at[h, pl.ds(pl.multiple_of(to * rows, rows), rows)], y_in.at[h, j],
+            y_send.at[h, j], y_recv.at[h, j], place(z, to, hi), s,
         )
 
     def z_copy(t):
@@ -258,9 +249,6 @@
             z_out.at[h], z_in.at[slot], z_send.at[slot], z_recv.at[slot], place(h, y, hi), s
         )
 
-    def own(h, block):
-        return part[h, pl.ds(pl.multiple_of(block * rows, rows), rows), :].astype(F32)
-
     def step(t, c):
         @pl.when((t < heads) & (s >= 1))
         def _():
@@ -294,12 +282,12 @@
             h = order(t - 1)
             att_copy(h).wait_recv()
             part[h] = dot(att[h], og2[...], 1, 0).astype(BF16)
-            y1_copy(h, 0).start()
-            y1_copy(h, 1).start()
-
-        @pl.when((s == 2) & (t >= 1) & (t <= heads))
-        def _():
-            h = order(t - 1)
+            for j in range(RING - 1):
+                y_copy(h, j).start()
+
+        @pl.when((s == 2) & (t >= 2) & (t <= heads + 1))
+        def _():
+            h = order(t - 2)
             back2(h).wait_recv()
             dkv_out[h, 0] = (
                 dkv_out[h, 0].astype(F32) + dkv_in[1, h].astype(F32)
@@ -318,46 +306,28 @@
             def _():
                 kv2(h).wait_send()
 
-            send_kv(t + AHEAD)
-
-        @pl.when(t == heads)
-        def _():
-            flat = att[:, :, 0:toks].reshape(heads * HEAD, toks).T
-
-            def project(i, cc):
-                at = pl.ds(pl.multiple_of(i * 512, 512), 512)
-                proj_out[:, at] = dot(flat, w[:, at], 1, 0).astype(BF16)
-                return cc
-
-            width = proj_out.shape[1]
-            if width >= 512:
-                lax.fori_loop(0, width // 512, project, 0)
-            else:
-                proj_out[...] = dot(flat, w[...], 1, 0).astype(BF16)
-
-        @pl.when((t >= 3) & (t <= heads + 2))
-        def _():
-            h = order(t - 3)
-            y1_copy(h, 0).wait_recv()
-            y1_copy(h, 1).wait_recv()
-            y1_sum[h] = (own(h, yb) + y1_in[h, 1].astype(F32)).astype(BF16)
-            y2_copy(h).start()
-
-        @pl.when(t >= 5)
-        def _():
-            h = order(t - 5)
-            y2_copy(h).wait_recv()
-            z_out[h] = (own(h, y) + y1_in[h, 0].astype(F32) + y2_in[h].astype(F32)).astype(BF16)
-
-            @pl.when(t < heads + 4)
-            def _():
-                z_copy(t - 5).start()
+            send_near(t + AHEAD)
+            send_far(t + AHEAD)
+
+        @pl.when(t >= LAG)
+        def _():
+            h = order(t - LAG)
+            for j in range(RING - 1):
+                y_copy(h, j).wait_recv()
+            whole = part[h, pl.ds(pl.multiple_of(y * rows, rows), rows), :].astype(F32)
+            for j in range(RING - 1):
+                whole = whole + y_in[h, j].astype(F32)
+            z_out[h] = whole.astype(BF16)
+
+            @pl.when(t < heads + LAG - 1)
+            def _():
+                z_copy(t - LAG).start()
 
         return c
 
     og2_copy.wait()
     ogs.wait_recv()
-    lax.fori_loop(0, heads + 5, step, 0)
+    lax.fori_loop(0, heads + LAG, step, 0)
 
     total = z_out[z].astype(F32)
     for t in range(PLANES - 1):
@@ -378,33 +348,16 @@
         copy.start()
         x_copies.append(copy)
 
-    def finish(h, c):
-        @pl.when(s < 3)
-        def _():
-            back1(h).wait_recv()
-
-        @pl.when(s == 0)
-        def _():
-            back2(h).wait_recv()
-
-        for i, out in enumerate((dk_out, dv_out)):
-            @pl.when(s == 3)
-            def _():
-                out[:, lanes(h)] = dkv_own[h, i].astype(BF16)
-
-            @pl.when((s == 1) | (s == 2))
-            def _():
-                out[:, lanes(h)] = (dkv_own[h, i] + dkv_in[0, h, i].astype(F32)).astype(BF16)
-
-            @pl.when(s == 0)
-            def _():
-                out[:, lanes(h)] = (
-                    dkv_own[h, i] + dkv_in[0, h, i].astype(F32) + dkv_in[1, h, i].astype(F32)
-                ).astype(BF16)
-
-        return c
-
-    lax.fori_loop(0, heads, finish, 0)
+    flat = att[:, :, 0:toks].reshape(heads * HEAD, toks).T
+    width = proj_out.shape[1]
+    span = min(512, width)
+
+    def project(i, c):
+        at = pl.ds(pl.multiple_of(i * span, span), span)
+        proj_out[:, at] = dot(flat, w[:, at], 1, 0).astype(BF16)
+        return c
+
+    lax.fori_loop(0, width // span, project, 0)
 
     result = x_out[pl.ds(pl.multiple_of(hi * share, share), share), :].astype(F32)
     for slot in range(len(targets)):
@@ -415,6 +368,34 @@
     last.start()
     wg_out[:, mine] = fin[...]
 
+    def finish(h, c):
+        @pl.when(s < 3)
+        def _():
+            back1(h).wait_recv()
+
+        @pl.when(s == 0)
+        def _():
+            back2(h).wait_recv()
+
+        for i, out in enumerate((dk_out, dv_out)):
+            @pl.when(s == 3)
+            def _():
+                out[:, lanes(h)] = dkv_own[h, i].astype(BF16)
+
+            @pl.when((s == 1) | (s == 2))
+            def _():
+                out[:, lanes(h)] = (dkv_own[h, i] + dkv_in[0, h, i].astype(F32)).astype(BF16)
+
+            @pl.when(s == 0)
+            def _():
+                out[:, lanes(h)] = (
+                    dkv_own[h, i] + dkv_in[0, h, i].astype(F32) + dkv_in[1, h, i].astype(F32)
+                ).astype(BF16)
+
+        return c
+
+    lax.fori_loop(0, heads, finish, 0)
+
     def drain(h, c):
         @pl.when((s < 3) & (h >= heads - AHEAD))
         def _():
@@ -437,9 +418,8 @@
             back2(h).wait_send()
 
         att_copy(h).wait_send()
-        y1_copy(h, 0).wait_send()
-        y1_copy(h, 1).wait_send()
-        y2_copy(h).wait_send()
+        for j in range(RING - 1):
+            y_copy(h, j).wait_send()
 
         @pl.when(h < heads - 1)
         def _():
@@ -517,9 +497,7 @@
             pltpu.VMEM((heads, 2, 2, toks, HEAD), BF16),
             pltpu.VMEM((2, heads, 2, toks, HEAD), BF16),
             pltpu.VMEM((heads, HEAD, cols), BF16),
-            pltpu.VMEM((heads, 2, rows, cols), BF16),
-            pltpu.VMEM((heads, rows, cols), BF16),
-            pltpu.VMEM((heads, rows, cols), BF16),
+            pltpu.VMEM((heads, RING - 1, rows, cols), BF16),
             pltpu.VMEM((heads, rows, cols), BF16),
             pltpu.VMEM((PLANES - 1, rows, cols), BF16),
             pltpu.VMEM((rows, cols), BF16),
@@ -529,8 +507,8 @@
             sem, sem((heads,)), sem, sem, sem, sem((2,)), sem((2,)), sem, sem,
             sem((heads,)), sem((heads,)), sem((heads,)), sem((heads,)),
             sem((heads,)), sem((heads,)), sem((heads,)), sem((heads,)),
-            sem((heads,)), sem((heads,)), sem((heads, 2)), sem((heads, 2)),
-            sem((heads,)), sem((heads,)), sem((PLANES - 1,)), sem((PLANES - 1,)),
+            sem((heads,)), sem((heads,)), sem((heads, RING - 1)), sem((heads, RING - 1)),
+            sem((PLANES - 1,)), sem((PLANES - 1,)),
             sem((3,)), sem((3,)), sem, sem,
         ],
         compiler_params=pltpu.CompilerParams(

time: 57.8 us -> 56.1 us (0.971)
  Pallas kernels: 57.1 us -> 55.3 us
    pallas_call x1, Pallas kernels: 55.5 us -> 53.8 us  [body(): pl.pallas_call(kernel, out_shape=(pltpu.VMEM((toks, width), BF16), pltpu....]
where the time goes in v3:
time: 56.1 us; the launch traced here: 56 us
  Pallas kernels  55.3 us (99%)
  between operations  0.64 us (1%)
    pallas_call x1, Pallas kernels, body(): pl.pallas_call(kernel, out_shape=(pltpu.VMEM((toks, width), BF16), pltpu....  53.8 us
    pallas_call x1, Pallas kernels, body(): pl.pallas_call(settle, out_shape=tuple((jax.ShapeDtypeStruct(out.shape, o...  1.54 us

profile of v3, /device:TPU:1, one launch (start us, length us, event | category | flops | bytes accessed | tf_op | source)
XLA Modules:
  0.0 56.0 jit_solution(11160779991144737877)
XLA Ops:
  0.6 53.8 %shard_map.101 = (bf16[256,2048]{1,0:T(8,128)(2,1)S(1)}, bf16[256,1024]{1,0:T(8,128)(2,1)S(1)}, bf16[256,1024]{1,0:T(8,128)(2,1)S(1)}, bf16[256,1024]{1,0:T(8,128)(2,1)S(1)}, bf16[16,2048]{1,0:T(8,128)(2,1)S(1)}) custom-call(bf16[256,1024]{1,0:T(8,128)(2,1)} %bitcast.10, bf16[256,1024]{1,0:T(8,128)(2,1)} %bitcast.11, bf16[256,1024]{1,0:T(8,128)(2,1)} %bitcast.12, ...), custom_call_target="tpu_custom_call" | custom-call | flops 8589934592 | bytes 10485760 | tf_op jit(solution)/shard_map/pallas_call | solution.py:474
  54.4 1.5 %shard_map.102 = (bf16[256,2048]{1,0:T(8,128)(2,1)}, bf16[256,1024]{1,0:T(8,128)(2,1)}, bf16[256,1024]{1,0:T(8,128)(2,1)}, bf16[256,1024]{1,0:T(8,128)(2,1)}, bf16[16,2048]{1,0:T(8,128)(2,1)}) custom-call(bf16[256,2048]{1,0:T(8,128)(2,1)S(1)} %get-tuple-element.15.refs_0_, bf16[256,1024]{1,0:T(8,128)(2,1)S(1)} %get-tuple-element.16.refs_1_, ...), custom_call_target="tpu_custom_call" | custom-call | tf_op jit(solution)/shard_map/pallas_call | solution.py:524

commit v4 on v3

--- a/solution.py
+++ b/solution.py
@@ -8,7 +8,7 @@
 HEAD = 128
 PLANES, RING, SIDES = 8, 4, 2
 AHEAD = 2
-LAG = 3
+LAG = 4
 MESH = pl.DeviceIdType.MESH
 F32, BF16 = jnp.float32, jnp.bfloat16
 LOG2E = 1.4426950408889634
@@ -22,11 +22,11 @@
     q_hbm, k_hbm, v_hbm, seg_ref, w_hbm, og_hbm,
     proj_out, dq_out, dk_out, dv_out, wg_out,
     q_s, kv, og, w, og2, dgrad, att, seg_own, seg_all, bias,
-    dkv_own, dkv_out, dkv_in, part, y_in, z_out, z_in, x_out, x_in, fin, fin_in,
+    dkv_own, dkv_out, dkv_in, part, y_in, z_out, z_in, x_out, x_in,
     q_sem, kv_sem, og_sem, w_sem, og2_sem, seg_send, seg_recv, ogs_send, ogs_recv,
     kv1_send, kv1_recv, kv2_send, kv2_recv, dk1_send, dk1_recv, dk2_send, dk2_recv,
     att_send, att_recv, y_send, y_recv, z_send, z_recv,
-    x_send, x_recv, f_send, f_recv,
+    x_send, x_recv,
 ):
     heads, toks = q_s.shape[0], q_s.shape[1]
     cols = og2.shape[1]
@@ -64,8 +64,7 @@
     peers = [(d, (s + 1) % 4), (d, (s + 2) % 4), (d, (s + 3) % 4)]
     peers += [(place(z, (y + i) % RING, hi), s) for i in range(1, RING)]
     peers += [(place((z + i) % PLANES, y, hi), s) for i in range(1, PLANES)]
-    if SIDES == 2:
-        peers += [(place(z, y, 1 - hi), core), (place(z, y, 1 - hi), 2 + core)]
+    peers += [(place(z, y, 1 - hi), i) for i in range(4)]
     for peer in peers:
         pl.semaphore_signal(barrier, inc=1, device_id=peer, device_id_type=MESH)
 
@@ -336,14 +335,14 @@
         total = total + z_in[slot].astype(F32)
     x_out[...] = total.astype(BF16)
     x_copies = []
-    targets = [(d, (1 - lo) * 2 + core, hi)]
-    if SIDES == 2:
-        targets += [(place(z, y, 1 - hi), core, 1 - hi), (place(z, y, 1 - hi), 2 + core, 1 - hi)]
-    for i, (dp, seq, part_of) in enumerate(targets):
-        slot = i if i == 0 else 1 + (i - 1 + lo) % 2
+    chip = hi * 2 + lo
+    for i in range(1, 8):
+        to = (chip + i // 2) % 4
+        to_core = (core + i % 2) % 2
+        piece = pl.ds(pl.multiple_of((to // 2) * share, share), share)
         copy = remote(
-            x_out.at[pl.ds(pl.multiple_of(part_of * share, share), share)], x_in.at[slot],
-            x_send.at[i], x_recv.at[slot], dp, seq,
+            x_out.at[piece], x_in.at[core, chip], x_send.at[i - 1], x_recv.at[core, chip],
+            place(z, y, to // 2), (to % 2) * 2 + to_core,
         )
         copy.start()
         x_copies.append(copy)
@@ -359,15 +358,7 @@
 
     lax.fori_loop(0, width // span, project, 0)
 
-    result = x_out[pl.ds(pl.multiple_of(hi * share, share), share), :].astype(F32)
-    for slot in range(len(targets)):
-        pltpu.make_async_copy(x_in.at[slot], x_in.at[slot], x_recv.at[slot]).wait()
-        result = result + x_in[slot].astype(F32)
-    fin[...] = result.astype(BF16)
-    last = remote(fin, fin_in, f_send, f_recv, d, sib)
-    last.start()
-    wg_out[:, mine] = fin[...]
-
+    x_in[core, chip] = x_out[pl.ds(pl.multiple_of(hi * share, share), share), :]
     def finish(h, c):
         @pl.when(s < 3)
         def _():
@@ -395,6 +386,15 @@
         return c
 
     lax.fori_loop(0, heads, finish, 0)
+    for i in range(1, 8):
+        piece = x_in.at[(core + i % 2) % 2, (chip + i // 2) % 4]
+        landed = x_recv.at[(core + i % 2) % 2, (chip + i // 2) % 4]
+        pltpu.make_async_copy(piece, piece, landed).wait()
+    for half in range(2):
+        result = x_in[half, 0].astype(F32)
+        for i in range(1, 4):
+            result = result + x_in[half, i].astype(F32)
+        wg_out[:, half * cols:(half + 1) * cols] = result.astype(BF16)
 
     def drain(h, c):
         @pl.when((s < 3) & (h >= heads - AHEAD))
@@ -439,9 +439,6 @@
     @pl.when(s < 2)
     def _():
         seg2.wait_send()
-
-    last.wait()
-    wg_out[:, other] = fin_in[...]
 
 
 def settle(*refs):
@@ -501,15 +498,13 @@
             pltpu.VMEM((heads, rows, cols), BF16),
             pltpu.VMEM((PLANES - 1, rows, cols), BF16),
             pltpu.VMEM((rows, cols), BF16),
-            pltpu.VMEM((3, share, cols), BF16),
-            pltpu.VMEM((share, cols), BF16),
-            pltpu.VMEM((share, cols), BF16),
+            pltpu.VMEM((2, 4, share, cols), BF16),
             sem, sem((heads,)), sem, sem, sem, sem((2,)), sem((2,)), sem, sem,
             sem((heads,)), sem((heads,)), sem((heads,)), sem((heads,)),
             sem((heads,)), sem((heads,)), sem((heads,)), sem((heads,)),
             sem((heads,)), sem((heads,)), sem((heads, RING - 1)), sem((heads, RING - 1)),
             sem((PLANES - 1,)), sem((PLANES - 1,)),
-            sem((3,)), sem((3,)), sem, sem,
+            sem((7,)), sem((2, 4)),
         ],
         compiler_params=pltpu.CompilerParams(
             collective_id=0, has_side_effects=True, vmem_limit_bytes=54 << 20

time: 56.1 us -> 55.4 us (0.988)
  Pallas kernels: 55.3 us -> 54.7 us
    pallas_call x1, Pallas kernels: 53.8 us -> 53.1 us  [body(): pl.pallas_call(kernel, out_shape=(pltpu.VMEM((toks, width), BF16), pltpu....]
where the time goes in v4:
time: 55.4 us; the launch traced here: 55.3 us
  Pallas kernels  54.7 us (99%)
  between operations  0.64 us (1%)
    pallas_call x1, Pallas kernels, body(): pl.pallas_call(kernel, out_shape=(pltpu.VMEM((toks, width), BF16), pltpu....  53.1 us
    pallas_call x1, Pallas kernels, body(): pl.pallas_call(settle, out_shape=tuple((jax.ShapeDtypeStruct(out.shape, o...  1.54 us

profile of v4, /device:TPU:1, one launch (start us, length us, event | category | flops | bytes accessed | tf_op | source)
XLA Modules:
  0.0 55.3 jit_solution(2238497930596905099)
XLA Ops:
  0.6 53.1 %shard_map.101 = (bf16[256,2048]{1,0:T(8,128)(2,1)S(1)}, bf16[256,1024]{1,0:T(8,128)(2,1)S(1)}, bf16[256,1024]{1,0:T(8,128)(2,1)S(1)}, bf16[256,1024]{1,0:T(8,128)(2,1)S(1)}, bf16[16,2048]{1,0:T(8,128)(2,1)S(1)}) custom-call(bf16[256,1024]{1,0:T(8,128)(2,1)} %bitcast.10, bf16[256,1024]{1,0:T(8,128)(2,1)} %bitcast.11, bf16[256,1024]{1,0:T(8,128)(2,1)} %bitcast.12, ...), custom_call_target="tpu_custom_call" | custom-call | flops 8589934592 | bytes 10485760 | tf_op jit(solution)/shard_map/pallas_call | solution.py:471
  53.8 1.5 %shard_map.102 = (bf16[256,2048]{1,0:T(8,128)(2,1)}, bf16[256,1024]{1,0:T(8,128)(2,1)}, bf16[256,1024]{1,0:T(8,128)(2,1)}, bf16[256,1024]{1,0:T(8,128)(2,1)}, bf16[16,2048]{1,0:T(8,128)(2,1)}) custom-call(bf16[256,2048]{1,0:T(8,128)(2,1)S(1)} %get-tuple-element.15.refs_0_, bf16[256,1024]{1,0:T(8,128)(2,1)S(1)} %get-tuple-element.16.refs_1_, ...), custom_call_target="tpu_custom_call" | custom-call | tf_op jit(solution)/shard_map/pallas_call | solution.py:519

commit v5 on v4

--- a/solution.py
+++ b/solution.py
@@ -7,7 +7,7 @@
 
 HEAD = 128
 PLANES, RING, SIDES = 8, 4, 2
-AHEAD = 2
+AHEAD = 3
 LAG = 4
 MESH = pl.DeviceIdType.MESH
 F32, BF16 = jnp.float32, jnp.bfloat16

time: 55.4 us -> 55.4 us (level)
  no operation moved by 1% of the time
where the time goes in v5:
time: 55.4 us; the launch traced here: 55.3 us
  Pallas kernels  54.7 us (99%)
  between operations  0.64 us (1%)
    pallas_call x1, Pallas kernels, body(): pl.pallas_call(kernel, out_shape=(pltpu.VMEM((toks, width), BF16), pltpu....  53.1 us
    pallas_call x1, Pallas kernels, body(): pl.pallas_call(settle, out_shape=tuple((jax.ShapeDtypeStruct(out.shape, o...  1.54 us

profile of v5, /device:TPU:1, one launch (start us, length us, event | category | flops | bytes accessed | tf_op | source)
XLA Modules:
  0.0 55.3 jit_solution(17618950056815007480)
XLA Ops:
  0.6 53.1 %shard_map.101 = (bf16[256,2048]{1,0:T(8,128)(2,1)S(1)}, bf16[256,1024]{1,0:T(8,128)(2,1)S(1)}, bf16[256,1024]{1,0:T(8,128)(2,1)S(1)}, bf16[256,1024]{1,0:T(8,128)(2,1)S(1)}, bf16[16,2048]{1,0:T(8,128)(2,1)S(1)}) custom-call(bf16[256,1024]{1,0:T(8,128)(2,1)} %bitcast.10, bf16[256,1024]{1,0:T(8,128)(2,1)} %bitcast.11, bf16[256,1024]{1,0:T(8,128)(2,1)} %bitcast.12, ...), custom_call_target="tpu_custom_call" | custom-call | flops 8589934592 | bytes 10485760 | tf_op jit(solution)/shard_map/pallas_call | solution.py:471
  53.8 1.5 %shard_map.102 = (bf16[256,2048]{1,0:T(8,128)(2,1)}, bf16[256,1024]{1,0:T(8,128)(2,1)}, bf16[256,1024]{1,0:T(8,128)(2,1)}, bf16[256,1024]{1,0:T(8,128)(2,1)}, bf16[16,2048]{1,0:T(8,128)(2,1)}) custom-call(bf16[256,2048]{1,0:T(8,128)(2,1)S(1)} %get-tuple-element.15.refs_0_, bf16[256,1024]{1,0:T(8,128)(2,1)S(1)} %get-tuple-element.16.refs_1_, ...), custom_call_target="tpu_custom_call" | custom-call | tf_op jit(solution)/shard_map/pallas_call | solution.py:519
